TPU v7x, 32 devices: a whole 2x2x4 slice. The times are simulated.
32 devices in a mesh: row: 4 (over x, core), col: 8 (over z, y).
Axes of the slice: x: 2, y: 2, z: 4, core: 2. Of those that a mesh axis runs over, the one named last changes fastest.
Arguments:
- contact: bfloat16 [256, 16384], P('row', 'col'), may hold values from -6 to 6
- first_down: bfloat16 [2, 3, 3, 32, 64], replicated, may hold values from -0.25 to 0.25
- first_down_bias: float32 [2, 32], replicated, may hold values from -1.5 to 1.5
- first_up: bfloat16 [2, 3, 3, 64, 32], replicated, may hold values from -0.375 to 0.375
- first_up_bias: float32 [2, 64], replicated, may hold values from -1.5 to 1.5
- second_down: bfloat16 [2, 3, 3, 32, 64], replicated, may hold values from -0.25 to 0.25
- second_down_bias: float32 [2, 32], replicated, may hold values from -1.5 to 1.5
- second_up: bfloat16 [2, 3, 3, 64, 32], replicated, may hold values from -0.375 to 0.375
- second_up_bias: float32 [2, 64], replicated, may hold values from -1.5 to 1.5
Outputs:
- decoded: bfloat16 [256, 16384], P('row', 'col')
All inputs are finite; a program needn't handle non-finite values.
Results may differ from a plain program's by a relative error of at most 0.012.
Values may be sent and summed in bfloat16 or wider, within the bound.
A program may use at most 64 MiB of HBM per device.

v0:
```python
import jax
import jax.numpy as jnp
from jax import lax
from jax.sharding import PartitionSpec as P


def with_halo(cells, sides, width):
    for axis, dim in sides:
        count = lax.axis_size(axis)
        ends = count - 1
        head = lax.slice_in_dim(cells, 0, width, axis=dim)
        tail = lax.slice_in_dim(cells, cells.shape[dim] - width, cells.shape[dim], axis=dim)
        cells = jnp.concatenate(
            [
                lax.ppermute(tail, axis, [(i, (i + 1) % count) for i in range(ends)]),
                cells,
                lax.ppermute(head, axis, [((i + 1) % count, i) for i in range(ends)]),
            ],
            axis=dim,
        )
    return cells


def conv_valid(source, weight, bias_term, dilation):
    out_rows = source.shape[1] - 2 * dilation
    out_cols = source.shape[2] - 2 * dilation
    summed = jnp.zeros((weight.shape[2], out_rows, out_cols), jnp.float32)
    for tap_row in range(3):
        for tap_col in range(3):
            window = source[
                :,
                tap_row * dilation : tap_row * dilation + out_rows,
                tap_col * dilation : tap_col * dilation + out_cols,
            ]
            summed = summed + jnp.einsum(
                "oc,crw->orw", weight[tap_row, tap_col], window, preferred_element_type=jnp.float32
            )
    return summed + bias_term[:, None, None]


def inside(margin, tile_rows, tile_cols):
    total_rows = tile_rows * lax.axis_size("row")
    total_cols = tile_cols * lax.axis_size("col")
    row_ids = (
        lax.axis_index("row") * tile_rows
        - margin
        + jnp.arange(tile_rows + 2 * margin, dtype=jnp.int32)
    )
    col_ids = (
        lax.axis_index("col") * tile_cols
        - margin
        + jnp.arange(tile_cols + 2 * margin, dtype=jnp.int32)
    )
    row_ok = (row_ids >= 0) & (row_ids < total_rows)
    col_ok = (col_ids >= 0) & (col_ids < total_cols)
    return (row_ok[:, None] & col_ok[None, :]).astype(jnp.float32)


def section_deep(field, down_weight, down_bias, up_weight, up_bias):
    tile_rows = field.shape[1]
    tile_cols = field.shape[2]
    margin = 15
    current = with_halo(field, (("row", 1), ("col", 2)), margin)
    for block_index, dilations in enumerate(((1, 2), (4, 8))):
        hidden_margin = margin - dilations[0]
        hidden = jax.nn.relu(
            conv_valid(current, down_weight[block_index], down_bias[block_index], dilations[0])
        )
        hidden = (hidden * inside(hidden_margin, tile_rows, tile_cols)).astype(jnp.bfloat16)
        out_margin = hidden_margin - dilations[1]
        update = conv_valid(hidden, up_weight[block_index], up_bias[block_index], dilations[1])
        trim = margin - out_margin
        base = current[:, trim : current.shape[1] - trim, trim : current.shape[2] - trim]
        current = (
            (base.astype(jnp.float32) + update) * inside(out_margin, tile_rows, tile_cols)
        ).astype(jnp.bfloat16)
        margin = out_margin
    return current


def run_section(field, down_weight, down_bias, up_weight, up_bias):
    return section_deep(field, down_weight, down_bias, up_weight, up_bias)


def mirrored(field):
    channels, tile_rows, tile_cols = field.shape
    col_count = lax.axis_size("col")
    row_count = lax.axis_size("row")
    pieces = field.reshape(channels, tile_rows // col_count, col_count, tile_cols)
    spread = lax.all_to_all(pieces, "col", split_axis=2, concat_axis=3, tiled=True)
    spread = spread.reshape(channels, tile_rows // col_count, row_count, tile_rows)
    arrived = lax.all_to_all(spread, "row", split_axis=2, concat_axis=1, tiled=True)
    arrived = arrived.reshape(channels, col_count, tile_cols // col_count, 1, tile_rows)
    settled = lax.all_to_all(arrived, "col", split_axis=1, concat_axis=3, tiled=True)
    return settled.reshape(channels, tile_cols, tile_rows).transpose(0, 2, 1)


def per_device(
    contact,
    first_down,
    first_down_bias,
    first_up,
    first_up_bias,
    second_down,
    second_down_bias,
    second_up,
    second_up_bias,
):
    channels = first_down.shape[4]
    tile_rows = contact.shape[0]
    tile_cols = contact.shape[1] // channels
    field = contact.reshape(tile_rows, tile_cols, channels).transpose(2, 0, 1)
    first = run_section(field, first_down, first_down_bias, first_up, first_up_bias)
    flipped = mirrored(first)
    symmetric = ((first.astype(jnp.float32) + flipped.astype(jnp.float32)) * 0.5).astype(
        jnp.bfloat16
    )
    result = run_section(symmetric, second_down, second_down_bias, second_up, second_up_bias)
    return result.transpose(1, 2, 0).reshape(tile_rows, tile_cols * channels)


def solution(mesh):
    in_specs = (P("row", "col"), P(), P(), P(), P(), P(), P(), P(), P())
    out_specs = P("row", "col")
    return jax.shard_map(
        per_device, mesh=mesh, in_specs=in_specs, out_specs=out_specs, check_vma=False
    )
```

profile of v0, /device:TPU:9, one launch (start us, length us, event | category | flops | bytes accessed | tf_op | source)
XLA Modules:
  0.0 123.0 jit_solution(3218191936298058240)
XLA Ops:
  0.0 1.3 %copy.53 = bf16[64,2048]{0,1:T(8,128)(2,1)S(1)} copy(bf16[64,2048]{1,0:T(8,128)(2,1)} %param.9) | data formatting | bytes 524288 | tf_op args[0]
  1.5 3.7 %collective-permute-start = (bf16[64,15,32]{1,0,2:T(8,128)(2,1)S(1)}, bf16[64,15,32]{1,0,2:T(8,128)(2,1)S(1)}, u32[]{:S(2)}, u32[]{:S(2)}) collective-permute-start(bf16[64,15,32]{1,0,2:T(8,128)(2,1)S(1)} %get-tuple-element.11), channel_id=1, source_target_pairs={{0,8},{8,16},{16,24},{1,9},{9,17},{17,25},{2,10},{10,18},{18,26},{... | collective-permute-start | bytes 184328 | tf_op jit(solution)/shard_map/ppermute | solution.py:15
  5.2 1.9 %collective-permute-start.1 = (bf16[64,15,32]{1,0,2:T(8,128)(2,1)S(1)}, bf16[64,15,32]{1,0,2:T(8,128)(2,1)S(1)}, u32[]{:S(2)}, u32[]{:S(2)}) collective-permute-start(bf16[64,15,32]{1,0,2:T(8,128)(2,1)S(1)} %get-tuple-element.12), channel_id=1, source_target_pairs={{8,0},{16,8},{24,16},{9,1},{17,9},{25,17},{10,2},{18,10},{26,18},{... | collective-permute-start | bytes 184328 | tf_op jit(solution)/shard_map/ppermute | solution.py:17
  7.7 3.7 %collective-permute-done = bf16[64,15,32]{1,0,2:T(8,128)(2,1)S(1)} collective-permute-done((bf16[64,15,32]{1,0,2:T(8,128)(2,1)S(1)}, bf16[64,15,32]{1,0,2:T(8,128)(2,1)S(1)}, u32[]{:S(2)}, u32[]{:S(2)}) %collective-permute-start) | collective-permute-done | bytes 61472 | tf_op jit(solution)/shard_map/ppermute | solution.py:15
  11.3 4.7 %collective-permute-done.1 = bf16[64,15,32]{1,0,2:T(8,128)(2,1)S(1)} collective-permute-done((bf16[64,15,32]{1,0,2:T(8,128)(2,1)S(1)}, bf16[64,15,32]{1,0,2:T(8,128)(2,1)S(1)}, u32[]{:S(2)}, u32[]{:S(2)}) %collective-permute-start.1) | collective-permute-done | bytes 61472 | tf_op jit(solution)/shard_map/ppermute | solution.py:17
  16.0 0.5 pad_maximum_fusion.7
  16.5 3.1 %collective-permute-start.2 = (bf16[64,94,15]{1,0,2:T(8,128)(2,1)S(1)}, bf16[64,94,15]{1,0,2:T(8,128)(2,1)S(1)}, u32[]{:S(2)}, u32[]{:S(2)}) collective-permute-start(bf16[64,94,15]{1,0,2:T(8,128)(2,1)S(1)} %get-tuple-element.7), channel_id=1, source_target_pairs={{0,1},{1,2},{2,3},{3,4},{4,5},{5,6},{6,7},{8,9},{9,10},{10,11},{11... | collective-permute-start | bytes 541448 | tf_op jit(solution)/shard_map/ppermute | solution.py:15
  19.6 3.0 %collective-permute-start.3 = (bf16[64,94,15]{1,0,2:T(8,128)(2,1)S(1)}, bf16[64,94,15]{1,0,2:T(8,128)(2,1)S(1)}, u32[]{:S(2)}, u32[]{:S(2)}) collective-permute-start(bf16[64,94,15]{1,0,2:T(8,128)(2,1)S(1)} %get-tuple-element.8), channel_id=1, source_target_pairs={{1,0},{2,1},{3,2},{4,3},{5,4},{6,5},{7,6},{9,8},{10,9},{11,10},{12... | collective-permute-start | bytes 541448 | tf_op jit(solution)/shard_map/ppermute | solution.py:17
  22.7 1.7 %collective-permute-done.2 = bf16[64,94,15]{1,0,2:T(8,128)(2,1)S(1)} collective-permute-done((bf16[64,94,15]{1,0,2:T(8,128)(2,1)S(1)}, bf16[64,94,15]{1,0,2:T(8,128)(2,1)S(1)}, u32[]{:S(2)}, u32[]{:S(2)}) %collective-permute-start.2) | collective-permute-done | bytes 180512 | tf_op jit(solution)/shard_map/ppermute | solution.py:15
  24.4 2.6 %collective-permute-done.3 = bf16[64,94,15]{1,0,2:T(8,128)(2,1)S(1)} collective-permute-done((bf16[64,94,15]{1,0,2:T(8,128)(2,1)S(1)}, bf16[64,94,15]{1,0,2:T(8,128)(2,1)S(1)}, u32[]{:S(2)}, u32[]{:S(2)}) %collective-permute-start.3) | collective-permute-done | bytes 180512 | tf_op jit(solution)/shard_map/ppermute | solution.py:17
  27.0 0.6 pad_maximum_fusion
  28.5 0.5 fusion.71
  29.8 0.5 fusion.77
  30.9 0.7 fusion.45
  31.6 0.5 fusion.128
  32.0 0.5 fusion.130
  32.5 0.5 fusion.132
  33.0 0.5 fusion.134
  33.5 0.5 fusion.136
  35.3 1.3 %fusion.3 = bf16[64,88,56]{1,0,2:T(8,128)(2,1)S(1)} fusion(f32[88,56,64]{0,2,1:T(8,128)S(1)} %fusion.128, f32[88,56,64]{0,2,1:T(8,128)S(1)} %fusion.130, f32[88,56,64]{0,2,1:T(8,128)S(1)} %fusion.132, f32[88,56,64]{0,2,1:T(8,128)S(1)} %fusion.134, f32[88,56,64]{0,2,1:T(8,128)S(1)} %fusion.136, f32[88,56,64]{0,2,1:T(8,128)S(1)} %fusion.138, ...), kind=kOutput, calls=%fused_computation.5 | convolution fusion | flops 24285184 | bytes 16724480 | tf_op jit(solution)/shard_map/oc,crw->orw/dot_general | solution.py:35
  40.8 0.6 convolution_add_fusion.13
  43.4 0.8 copy.63
  44.6 10.4 %all_to_all.33 = bf16[8,2,8192]{2,1,0:T(2,128)(2,1)S(1)} all-to-all(bf16[8,2,8192]{2,1,0:T(2,128)(2,1)S(1)} %reshape.281), channel_id=1, replica_groups=mesh['row'=4,'col'=8] {'col'}, dimensions={0} | all-to-all | bytes 524288 | tf_op jit(solution)/shard_map/all_to_all | solution.py:90
  55.8 9.0 %all_to_all.34 = bf16[4,2,16384]{2,1,0:T(2,128)(2,1)S(1)} all-to-all(bf16[4,2,16384]{2,1,0:T(2,128)(2,1)S(1)} %reshape.283), channel_id=1, replica_groups=mesh['row'=4,'col'=8] {'row'}, dimensions={0} | all-to-all | bytes 524288 | tf_op jit(solution)/shard_map/all_to_all | solution.py:92
  65.5 1.1 reshape.285
  66.5 5.1 %all-to-all-start.2 = ((bf16[8,2,8192]{2,1,0:T(2,128)(2,1)}), bf16[8,2,8192]{2,1,0:T(2,128)(2,1)S(1)}, u32[]{:S(2)}, u32[]{:S(2)}) async-start(bf16[8,2,8192]{2,1,0:T(2,128)(2,1)} %reshape.285), calls=%async_computation.2 | async-start | bytes 524288 | tf_op jit(solution)/shard_map/all_to_all | solution.py:94
  71.6 6.2 %all-to-all-done.2 = bf16[8,2,8192]{2,1,0:T(2,128)(2,1)S(1)} async-done(((bf16[8,2,8192]{2,1,0:T(2,128)(2,1)}), bf16[8,2,8192]{2,1,0:T(2,128)(2,1)S(1)}, u32[]{:S(2)}, u32[]{:S(2)}) %all-to-all-start.2) | async-done | bytes 262176 | tf_op jit(solution)/shard_map/all_to_all | solution.py:94
  78.8 5.3 %collective-permute-start.4 = (bf16[64,15,32]{1,0,2:T(8,128)(2,1)S(1)}, bf16[64,15,32]{1,0,2:T(8,128)(2,1)S(1)}, u32[]{:S(2)}, u32[]{:S(2)}) collective-permute-start(bf16[64,15,32]{1,0,2:T(8,128)(2,1)S(1)} %get-tuple-element.9), channel_id=1, source_target_pairs={{0,8},{8,16},{16,24},{1,9},{9,17},{17,25},{2,10},{10,18},{18,26},{... | collective-permute-start | bytes 184328 | tf_op jit(solution)/shard_map/ppermute | solution.py:15
  84.2 1.9 %collective-permute-start.5 = (bf16[64,15,32]{1,0,2:T(8,128)(2,1)S(1)}, bf16[64,15,32]{1,0,2:T(8,128)(2,1)S(1)}, u32[]{:S(2)}, u32[]{:S(2)}) collective-permute-start(bf16[64,15,32]{1,0,2:T(8,128)(2,1)S(1)} %get-tuple-element.10), channel_id=1, source_target_pairs={{8,0},{16,8},{24,16},{9,1},{17,9},{25,17},{10,2},{18,10},{26,18},{... | collective-permute-start | bytes 184328 | tf_op jit(solution)/shard_map/ppermute | solution.py:17
  86.1 4.2 %collective-permute-done.4 = bf16[64,15,32]{1,0,2:T(8,128)(2,1)S(1)} collective-permute-done((bf16[64,15,32]{1,0,2:T(8,128)(2,1)S(1)}, bf16[64,15,32]{1,0,2:T(8,128)(2,1)S(1)}, u32[]{:S(2)}, u32[]{:S(2)}) %collective-permute-start.4) | collective-permute-done | bytes 61472 | tf_op jit(solution)/shard_map/ppermute | solution.py:15
  90.3 4.7 %collective-permute-done.5 = bf16[64,15,32]{1,0,2:T(8,128)(2,1)S(1)} collective-permute-done((bf16[64,15,32]{1,0,2:T(8,128)(2,1)S(1)}, bf16[64,15,32]{1,0,2:T(8,128)(2,1)S(1)}, u32[]{:S(2)}, u32[]{:S(2)}) %collective-permute-start.5) | collective-permute-done | bytes 61472 | tf_op jit(solution)/shard_map/ppermute | solution.py:17
  95.0 0.5 pad_maximum_fusion.4
  95.4 2.1 %collective-permute-start.6 = (bf16[64,94,15]{1,0,2:T(8,128)(2,1)S(1)}, bf16[64,94,15]{1,0,2:T(8,128)(2,1)S(1)}, u32[]{:S(2)}, u32[]{:S(2)}) collective-permute-start(bf16[64,94,15]{1,0,2:T(8,128)(2,1)S(1)} %get-tuple-element.5), channel_id=1, source_target_pairs={{0,1},{1,2},{2,3},{3,4},{4,5},{5,6},{6,7},{8,9},{9,10},{10,11},{11... | collective-permute-start | bytes 541448 | tf_op jit(solution)/shard_map/ppermute | solution.py:15
  97.5 4.1 %collective-permute-start.7 = (bf16[64,94,15]{1,0,2:T(8,128)(2,1)S(1)}, bf16[64,94,15]{1,0,2:T(8,128)(2,1)S(1)}, u32[]{:S(2)}, u32[]{:S(2)}) collective-permute-start(bf16[64,94,15]{1,0,2:T(8,128)(2,1)S(1)} %get-tuple-element.6), channel_id=1, source_target_pairs={{1,0},{2,1},{3,2},{4,3},{5,4},{6,5},{7,6},{9,8},{10,9},{11,10},{12... | collective-permute-start | bytes 541448 | tf_op jit(solution)/shard_map/ppermute | solution.py:17
  101.6 1.7 %collective-permute-done.6 = bf16[64,94,15]{1,0,2:T(8,128)(2,1)S(1)} collective-permute-done((bf16[64,94,15]{1,0,2:T(8,128)(2,1)S(1)}, bf16[64,94,15]{1,0,2:T(8,128)(2,1)S(1)}, u32[]{:S(2)}, u32[]{:S(2)}) %collective-permute-start.6) | collective-permute-done | bytes 180512 | tf_op jit(solution)/shard_map/ppermute | solution.py:15
  103.4 2.5 %collective-permute-done.7 = bf16[64,94,15]{1,0,2:T(8,128)(2,1)S(1)} collective-permute-done((bf16[64,94,15]{1,0,2:T(8,128)(2,1)S(1)}, bf16[64,94,15]{1,0,2:T(8,128)(2,1)S(1)}, u32[]{:S(2)}, u32[]{:S(2)}) %collective-permute-start.7) | collective-permute-done | bytes 180512 | tf_op jit(solution)/shard_map/ppermute | solution.py:17
  105.9 0.6 pad_maximum_fusion.1
  107.4 0.5 fusion.54
  107.9 0.5 fusion.56
  108.3 0.5 fusion.58
  109.8 0.7 fusion.44
  110.5 0.5 fusion.108
  111.0 0.5 fusion.110
  111.5 0.5 fusion.112
  111.9 0.5 fusion.114
  112.4 0.5 fusion.116
  114.2 1.3 %fusion.1 = bf16[64,88,56]{1,0,2:T(8,128)(2,1)S(1)} fusion(f32[88,56,64]{0,2,1:T(8,128)S(1)} %fusion.108, f32[88,56,64]{0,2,1:T(8,128)S(1)} %fusion.110, f32[88,56,64]{0,2,1:T(8,128)S(1)} %fusion.112, f32[88,56,64]{0,2,1:T(8,128)S(1)} %fusion.114, f32[88,56,64]{0,2,1:T(8,128)S(1)} %fusion.116, f32[88,56,64]{0,2,1:T(8,128)S(1)} %fusion.118, ...), kind=kOutput, calls=%fused_computation.2 | convolution fusion | flops 24285184 | bytes 16724480 | tf_op jit(solution)/shard_map/oc,crw->orw/dot_general | solution.py:35
  122.1 0.9 copy.79
  (102 shorter events, 23.1 us)
Async XLA Ops:
  0.0 7.2 %copy-start = (bf16[2,3,3,32,64]{4,3,2,1,0:T(8,128)(2,1)S(1)}, bf16[2,3,3,32,64]{4,3,2,1,0:T(8,128)(2,1)}, u32[]{:S(2)}) copy-start(bf16[2,3,3,32,64]{4,3,2,1,0:T(8,128)(2,1)} %param.10) | copy-start | bytes 221188
  0.0 7.3 %copy-start.1 = (bf16[2,3,3,64,32]{3,4,2,1,0:T(8,128)(2,1)S(1)}, bf16[2,3,3,64,32]{3,4,2,1,0:T(8,128)(2,1)}, u32[]{:S(2)}) copy-start(bf16[2,3,3,64,32]{3,4,2,1,0:T(8,128)(2,1)} %param.12) | copy-start | bytes 221188
  0.0 7.7 %copy-start.4 = (f32[2,32]{1,0:T(2,128)S(1)}, f32[2,32]{1,0:T(2,128)}, u32[]{:S(2)}) copy-start(f32[2,32]{1,0:T(2,128)} %param.11) | copy-start | bytes 772
  1.5 21.2 %copy-start.5 = (f32[2,64]{1,0:T(2,128)S(1)}, f32[2,64]{1,0:T(2,128)}, u32[]{:S(2)}) copy-start(f32[2,64]{1,0:T(2,128)} %param.13) | copy-start | bytes 1540
  1.5 9.8 %collective-permute-start = (bf16[64,15,32]{1,0,2:T(8,128)(2,1)S(1)}, bf16[64,15,32]{1,0,2:T(8,128)(2,1)S(1)}, u32[]{:S(2)}, u32[]{:S(2)}) collective-permute-start(bf16[64,15,32]{1,0,2:T(8,128)(2,1)S(1)} %get-tuple-element.11), channel_id=1, source_target_pairs={{0,8},{8,16},{16,24},{1,9},{9,17},{17,25},{2,10},{10,18},{18,26},{... | collective-permute-start | bytes 184328 | tf_op jit(solution)/shard_map/ppermute | solution.py:15
  5.2 10.8 %collective-permute-start.1 = (bf16[64,15,32]{1,0,2:T(8,128)(2,1)S(1)}, bf16[64,15,32]{1,0,2:T(8,128)(2,1)S(1)}, u32[]{:S(2)}, u32[]{:S(2)}) collective-permute-start(bf16[64,15,32]{1,0,2:T(8,128)(2,1)S(1)} %get-tuple-element.12), channel_id=1, source_target_pairs={{8,0},{16,8},{24,16},{9,1},{17,9},{25,17},{10,2},{18,10},{26,18},{... | collective-permute-start | bytes 184328 | tf_op jit(solution)/shard_map/ppermute | solution.py:17
  16.5 7.9 %collective-permute-start.2 = (bf16[64,94,15]{1,0,2:T(8,128)(2,1)S(1)}, bf16[64,94,15]{1,0,2:T(8,128)(2,1)S(1)}, u32[]{:S(2)}, u32[]{:S(2)}) collective-permute-start(bf16[64,94,15]{1,0,2:T(8,128)(2,1)S(1)} %get-tuple-element.7), channel_id=1, source_target_pairs={{0,1},{1,2},{2,3},{3,4},{4,5},{5,6},{6,7},{8,9},{9,10},{10,11},{11... | collective-permute-start | bytes 541448 | tf_op jit(solution)/shard_map/ppermute | solution.py:15
  19.6 7.3 %collective-permute-start.3 = (bf16[64,94,15]{1,0,2:T(8,128)(2,1)S(1)}, bf16[64,94,15]{1,0,2:T(8,128)(2,1)S(1)}, u32[]{:S(2)}, u32[]{:S(2)}) collective-permute-start(bf16[64,94,15]{1,0,2:T(8,128)(2,1)S(1)} %get-tuple-element.8), channel_id=1, source_target_pairs={{1,0},{2,1},{3,2},{4,3},{5,4},{6,5},{7,6},{9,8},{10,9},{11,10},{12... | collective-permute-start | bytes 541448 | tf_op jit(solution)/shard_map/ppermute | solution.py:17
  55.8 15.8 %copy-start.2 = (bf16[2,3,3,32,64]{4,3,2,1,0:T(8,128)(2,1)S(1)}, bf16[2,3,3,32,64]{4,3,2,1,0:T(8,128)(2,1)}, u32[]{:S(2)}) copy-start(bf16[2,3,3,32,64]{4,3,2,1,0:T(8,128)(2,1)} %param.14) | copy-start | bytes 221188
  64.8 6.8 %copy-start.3 = (bf16[2,3,3,64,32]{3,4,2,1,0:T(8,128)(2,1)S(1)}, bf16[2,3,3,64,32]{3,4,2,1,0:T(8,128)(2,1)}, u32[]{:S(2)}) copy-start(bf16[2,3,3,64,32]{3,4,2,1,0:T(8,128)(2,1)} %param.16) | copy-start | bytes 221188
  66.5 11.3 %all-to-all-start.2 = ((bf16[8,2,8192]{2,1,0:T(2,128)(2,1)}), bf16[8,2,8192]{2,1,0:T(2,128)(2,1)S(1)}, u32[]{:S(2)}, u32[]{:S(2)}) async-start(bf16[8,2,8192]{2,1,0:T(2,128)(2,1)} %reshape.285), calls=%async_computation.2 | async-start | bytes 524288 | tf_op jit(solution)/shard_map/all_to_all | solution.py:94
  78.4 7.7 %copy-start.6 = (f32[2,32]{1,0:T(2,128)S(1)}, f32[2,32]{1,0:T(2,128)}, u32[]{:S(2)}) copy-start(f32[2,32]{1,0:T(2,128)} %param.15) | copy-start | bytes 772
  78.5 23.1 %copy-start.7 = (f32[2,64]{1,0:T(2,128)S(1)}, f32[2,64]{1,0:T(2,128)}, u32[]{:S(2)}) copy-start(f32[2,64]{1,0:T(2,128)} %param.17) | copy-start | bytes 1540
  78.8 11.5 %collective-permute-start.4 = (bf16[64,15,32]{1,0,2:T(8,128)(2,1)S(1)}, bf16[64,15,32]{1,0,2:T(8,128)(2,1)S(1)}, u32[]{:S(2)}, u32[]{:S(2)}) collective-permute-start(bf16[64,15,32]{1,0,2:T(8,128)(2,1)S(1)} %get-tuple-element.9), channel_id=1, source_target_pairs={{0,8},{8,16},{16,24},{1,9},{9,17},{17,25},{2,10},{10,18},{18,26},{... | collective-permute-start | bytes 184328 | tf_op jit(solution)/shard_map/ppermute | solution.py:15
  84.2 10.8 %collective-permute-start.5 = (bf16[64,15,32]{1,0,2:T(8,128)(2,1)S(1)}, bf16[64,15,32]{1,0,2:T(8,128)(2,1)S(1)}, u32[]{:S(2)}, u32[]{:S(2)}) collective-permute-start(bf16[64,15,32]{1,0,2:T(8,128)(2,1)S(1)} %get-tuple-element.10), channel_id=1, source_target_pairs={{8,0},{16,8},{24,16},{9,1},{17,9},{25,17},{10,2},{18,10},{26,18},{... | collective-permute-start | bytes 184328 | tf_op jit(solution)/shard_map/ppermute | solution.py:17
  95.4 7.9 %collective-permute-start.6 = (bf16[64,94,15]{1,0,2:T(8,128)(2,1)S(1)}, bf16[64,94,15]{1,0,2:T(8,128)(2,1)S(1)}, u32[]{:S(2)}, u32[]{:S(2)}) collective-permute-start(bf16[64,94,15]{1,0,2:T(8,128)(2,1)S(1)} %get-tuple-element.5), channel_id=1, source_target_pairs={{0,1},{1,2},{2,3},{3,4},{4,5},{5,6},{6,7},{8,9},{9,10},{10,11},{11... | collective-permute-start | bytes 541448 | tf_op jit(solution)/shard_map/ppermute | solution.py:15
  97.5 8.4 %collective-permute-start.7 = (bf16[64,94,15]{1,0,2:T(8,128)(2,1)S(1)}, bf16[64,94,15]{1,0,2:T(8,128)(2,1)S(1)}, u32[]{:S(2)}, u32[]{:S(2)}) collective-permute-start(bf16[64,94,15]{1,0,2:T(8,128)(2,1)S(1)} %get-tuple-element.6), channel_id=1, source_target_pairs={{1,0},{2,1},{3,2},{4,3},{5,4},{6,5},{7,6},{9,8},{10,9},{11,10},{12... | collective-permute-start | bytes 541448 | tf_op jit(solution)/shard_map/ppermute | solution.py:17
where the time goes:
time: 124 us; the launch traced here: 123 us
  waiting for transfers between devices  31.9 us (26%)
  matrix products  31.1 us (25%)
  starting transfers between devices  30.3 us (24%)
  blocking collectives  19.4 us (16%)
  local copies, waits for them, and re-layouts  6.91 us (6%)
  other arithmetic  2.78 us (2%)
    dot_general x72, matrix products, conv_valid(): jnp.einsum('oc,crw->orw', weight[tap_row, tap_col], window, preferred_ele...  31.1 us
    ppermute x4, waiting for transfers between devices, with_halo(): lax.ppermute(head, axis, [((i + 1) % count, i) for i in range(ends)])  14.5 us
    ppermute x4, starting transfers between devices, with_halo(): lax.ppermute(tail, axis, [(i, (i + 1) % count) for i in range(ends)])  14.2 us
    ppermute x4, waiting for transfers between devices, with_halo(): lax.ppermute(tail, axis, [(i, (i + 1) % count) for i in range(ends)])  11.2 us
    ppermute x4, starting transfers between devices, with_halo(): lax.ppermute(head, axis, [((i + 1) % count, i) for i in range(ends)])  11 us
    all_to_all x1, blocking collectives, mirrored(): lax.all_to_all(pieces, 'col', split_axis=2, concat_axis=3, tiled=True)  10.4 us
    all_to_all x1, blocking collectives, mirrored(): lax.all_to_all(spread, 'row', split_axis=2, concat_axis=1, tiled=True)  9 us
    all_to_all x1, waiting for transfers between devices, mirrored(): lax.all_to_all(arrived, 'col', split_axis=1, concat_axis=3, tiled=True)  6.16 us
  transfers between devices with their start and end apart: 9, of which 9 were waited for; matrix products, arithmetic and copies ran while one was open for 0% of the time, Pallas kernels for 0%

commit v1 on v0

v1 whole, which is shorter than its diff:
```python
import functools

import jax
import jax.numpy as jnp
from jax import lax
from jax.experimental import pallas as pl
from jax.experimental.pallas import tpu as pltpu
from jax.sharding import PartitionSpec as P

MESH = pl.DeviceIdType.MESH
HALO = 16
SIDE = HALO // 2
BLOCKS = ((1, 2), (4, 8))
WAYS = ((0, -1), (0, 1), (-1, 0), (1, 0), (-1, -1), (-1, 1), (1, -1), (1, 1))
NT = (((1,), (1,)), ((), ()))


def chunk_of(count, most):
    return max(n for n in range(1, most + 1) if count % n == 0)


def kernel(
    rows_of, cols_of,
    contact, fd, fdb, fu, fub, sd, sdb, su, sub,
    out,
    v1, v2, hid, mirror, wide, flipped, wd, wu, bias,
    send1, recv1, send2, recv2, send_m, recv_m, local_sem,
):
    tile_rows = contact.shape[0]
    pairs = contact.shape[1] // 128
    span = tile_rows + 2 * HALO
    all_pairs = pairs + 2 * SIDE
    square = 2 * pairs
    fold = tile_rows // square
    r = lax.axis_index("row")
    c = lax.axis_index("col")
    up_edge, down_edge = r == 0, r == rows_of - 1
    left_edge, right_edge = c == 0, c == cols_of - 1

    def there(dr, dc):
        return (r + dr >= 0) & (r + dr < rows_of) & (c + dc >= 0) & (c + dc < cols_of)

    mirror_row = lax.div(c, fold)
    peers = [(mirror_row, fold * r + m) for m in range(fold)]
    slot = lax.rem(c, fold)

    def is_me(peer):
        return (peer[0] == r) & (peer[1] == c)

    barrier = pltpu.get_barrier_semaphore()
    greeted = jnp.int32(0)
    for dr, dc in WAYS:
        ok = there(dr, dc)
        greeted += ok.astype(jnp.int32)

        @pl.when(ok)
        def _():
            pl.semaphore_signal(barrier, inc=1, device_id=(r + dr, c + dc), device_id_type=MESH)

    for peer in peers:
        other = jnp.logical_not(is_me(peer))
        greeted += other.astype(jnp.int32)

        @pl.when(other)
        def _():
            pl.semaphore_signal(barrier, inc=1, device_id=peer, device_id_type=MESH)

    def clear(buf, first, last, lanes=slice(None)):
        rows = buf.shape[1]
        width = 128 if lanes == slice(None) else 64
        buf[first:last, :, lanes] = jnp.zeros((last - first, rows, width), buf.dtype)

    def clear_rows(buf):
        strip = jnp.zeros((all_pairs, HALO, 128), buf.dtype)

        @pl.when(up_edge)
        def _():
            buf[:, 0:HALO, :] = strip

        @pl.when(down_edge)
        def _():
            buf[:, HALO + tile_rows : span, :] = strip

    def clear_outside(buf):
        clear_rows(buf)

        @pl.when(left_edge)
        def _():
            clear(buf, 0, SIDE)

        @pl.when(right_edge)
        def _():
            clear(buf, SIDE + pairs, all_pairs)

    def clear_hidden(s):
        clear_rows(hid)

        @pl.when(left_edge)
        def _():
            clear(hid, 0, SIDE, slice(0, 64))
            clear(hid, 0, SIDE - s, slice(64, 128))

        @pl.when(right_edge)
        def _():
            clear(hid, SIDE + pairs, all_pairs, slice(0, 64))
            clear(hid, SIDE + pairs - s, all_pairs, slice(64, 128))

    def halo_copies(buf, send, recv):
        copies = []
        for at, (dr, dc) in enumerate(WAYS):
            src_row = {-1: (HALO, HALO), 0: (HALO, tile_rows), 1: (tile_rows, HALO)}[dr]
            dst_row = {-1: HALO + tile_rows, 0: HALO, 1: 0}[dr]
            src_col = {-1: (SIDE, SIDE), 0: (SIDE, pairs), 1: (pairs, SIDE)}[dc]
            dst_col = {-1: SIDE + pairs, 0: SIDE, 1: 0}[dc]
            copies.append(
                pltpu.make_async_remote_copy(
                    src_ref=buf.at[pl.ds(*src_col), pl.ds(*src_row), :],
                    dst_ref=buf.at[pl.ds(dst_col, src_col[1]), pl.ds(dst_row, src_row[1]), :],
                    send_sem=send.at[at],
                    recv_sem=recv.at[at],
                    device_id=(jnp.clip(r + dr, 0, rows_of - 1), jnp.clip(c + dc, 0, cols_of - 1)),
                    device_id_type=MESH,
                )
            )
        return copies

    def start_halo(copies):
        for (dr, dc), copy in zip(WAYS, copies):
            pl.when(there(dr, dc))(copy.start)

    def finish_halo(copies):
        for (dr, dc), copy in zip(WAYS, copies):
            pl.when(there(-dr, -dc))(copy.wait_recv)
        for (dr, dc), copy in zip(WAYS, copies):
            pl.when(there(dr, dc))(copy.wait_send)

    def down(buf, at, d, s, s_up, low, high):
        n = chunk_of(high - low, 8)

        def step(i, carry):
            j = low + i * n
            x = jnp.concatenate(
                [buf[pl.ds(j - s, n)], buf[pl.ds(j, n)], buf[pl.ds(j + s, n)]], axis=-1
            ).reshape(n * span, 384)
            sums = lax.dot_general(x, wd[at], NT, preferred_element_type=jnp.float32)
            outer, middle = sums[:, :128], sums[:, 128:]
            h = pltpu.roll(outer, d, 0) + middle
            h = h + pltpu.roll(pltpu.roll(outer, 64, 1), n * span - d, 0)
            h = jnp.maximum(h + bias[at : at + 1, :], 0.0)
            moved = pltpu.roll(h, 64, 1)
            hid[pl.ds(j, n), :, 0:64] = h.astype(jnp.bfloat16).reshape(n, span, 128)[:, :, 0:64]
            hid[pl.ds(j - s_up, n), :, 64:128] = moved.astype(jnp.bfloat16).reshape(n, span, 128)[
                :, :, 64:128
            ]
            return carry

        lax.fori_loop(0, (high - low) // n, step, 0)

    def up(buf, at, d, s, low, high, store):
        n = chunk_of(high - low, 8)

        def step(i, carry):
            j = low + i * n
            x = jnp.concatenate([hid[pl.ds(j - s, n)], hid[pl.ds(j + s, n)]], axis=-1)
            sums = lax.dot_general(
                x.reshape(n * span, 256), wu[at], NT, preferred_element_type=jnp.float32
            )
            u = pltpu.roll(sums[:, :128], d, 0) + sums[:, 128:256]
            u = u + pltpu.roll(sums[:, 256:], n * span - d, 0)
            u = (u + bias[4 + at : 5 + at, :]).reshape(n, span, 128)
            store(j, n, u)
            return carry

        lax.fori_loop(0, (high - low) // n, step, 0)

    def section(buf, first_at, store_last):
        margin = 2 * SIDE
        used = 0
        for block, (d1, d2) in enumerate(BLOCKS):
            at = first_at + block
            s1, s2 = max(d1 // 2, 1), d2 // 2
            used += s1
            down(buf, at, d1, s1, s2, used, all_pairs - used)
            clear_hidden(s2)
            used += s2
            last = block == len(BLOCKS) - 1

            def store(j, n, u):
                v = buf[pl.ds(j, n)].astype(jnp.float32) + u
                buf[pl.ds(j, n)] = v.astype(jnp.bfloat16)

            up(buf, at, d2, s2, used, all_pairs - used, store_last if last else store)
            if not last:
                clear_outside(buf)

    for j in range(pairs):
        v1[SIDE + j, HALO : HALO + tile_rows, :] = contact[:, 128 * j : 128 * (j + 1)]
    pl.semaphore_wait(barrier, greeted)
    first_halo = halo_copies(v1, send1, recv1)
    start_halo(first_halo)

    clear_outside(v1)
    clear_outside(v2)
    hid[...] = jnp.zeros(hid.shape, hid.dtype)
    wd[...] = jnp.zeros(wd.shape, wd.dtype)
    wu[...] = jnp.zeros(wu.shape, wu.dtype)
    bias[...] = jnp.zeros(bias.shape, bias.dtype)
    for sec, (dw, db, uw, ub) in enumerate(((fd, fdb, fu, fub), (sd, sdb, su, sub))):
        for block, (d1, d2) in enumerate(BLOCKS):
            at = 2 * sec + block
            bias[at : at + 1, 0:32] = db[block : block + 1, :]
            bias[at : at + 1, 32:64] = db[block : block + 1, :]
            bias[4 + at : 5 + at, 0:64] = ub[block : block + 1, :]
            bias[4 + at : 5 + at, 64:128] = ub[block : block + 1, :]
            for p in range(3):
                group = (0, 128, 64)[p]
                for q in range(3):
                    for par in range(2):
                        shift = par + (q - 1) * d1
                        third = 1 + (shift // 2 > 0) - (shift // 2 < 0)
                        lane = third * 128 + (shift % 2) * 64
                        row = group + par * 32
                        wd[at, row : row + 32, lane : lane + 64] = dw[block, p, q]
                        row = p * 128 + par * 64
                        lane = q * 64 + par * 32
                        wu[at, row : row + 64, lane : lane + 32] = uw[block, p, q]

    finish_halo(first_halo)

    def store_first(j, n, u):
        inner = slice(HALO, HALO + tile_rows)
        v = v1[pl.ds(j, n), inner, :].astype(jnp.float32) + u[:, inner, :]
        v1[pl.ds(j, n), inner, :] = v.astype(jnp.bfloat16)

    section(v1, 0, store_first)

    mirrors = []
    for m, peer in enumerate(peers):
        src = v1.at[pl.ds(SIDE, pairs), pl.ds(HALO + m * square, square), :]
        remote = pltpu.make_async_remote_copy(
            src_ref=src,
            dst_ref=mirror.at[slot],
            send_sem=send_m.at[m],
            recv_sem=recv_m.at[slot],
            device_id=peer,
            device_id_type=MESH,
        )
        here = pltpu.make_async_copy(src, mirror.at[slot], local_sem)
        mirrors.append((peer, remote, here))
        pl.when(jnp.logical_not(is_me(peer)))(remote.start)
        pl.when(is_me(peer))(here.start)
    for m, (peer, remote, here) in enumerate(mirrors):
        arrived = pltpu.make_async_remote_copy(
            src_ref=mirror.at[m],
            dst_ref=mirror.at[m],
            send_sem=send_m.at[m],
            recv_sem=recv_m.at[m],
            device_id=peer,
            device_id_type=MESH,
        )
        pl.when(jnp.logical_not(is_me(peer)))(arrived.wait_recv)
        pl.when(is_me(peer))(here.wait)
    low_half = lax.broadcasted_iota(jnp.int32, (pairs, 128), 1) < 64
    for m in range(fold):
        wide[...] = mirror[m].astype(jnp.float32).reshape(pairs * square, 128)
        for j in range(pairs):
            even = wide[pl.ds(2 * j, pairs, stride=square), :]
            odd = wide[pl.ds(2 * j + 1, pairs, stride=square), :]
            base = j * tile_rows + m * square
            flipped[pl.ds(base, pairs, stride=2), :] = jnp.where(
                low_half, even, pltpu.roll(odd, 64, 1)
            )
            flipped[pl.ds(base + 1, pairs, stride=2), :] = jnp.where(
                low_half, pltpu.roll(even, 64, 1), odd
            )
    own = v1[SIDE : SIDE + pairs, HALO : HALO + tile_rows, :].astype(jnp.float32)
    both = (own + flipped[...].reshape(pairs, tile_rows, 128)) * 0.5
    v2[SIDE : SIDE + pairs, HALO : HALO + tile_rows, :] = both.astype(jnp.bfloat16)

    second_halo = halo_copies(v2, send2, recv2)
    start_halo(second_halo)
    for peer, remote, here in mirrors:
        pl.when(jnp.logical_not(is_me(peer)))(remote.wait_send)
    finish_halo(second_halo)

    def store_second(j, n, u):
        inner = slice(HALO, HALO + tile_rows)
        v = (v2[pl.ds(j, n), inner, :].astype(jnp.float32) + u[:, inner, :]).astype(jnp.bfloat16)
        for k in range(n):
            out[:, pl.ds(pl.multiple_of((j - SIDE + k) * 128, 128), 128)] = v[k]

    section(v2, 2, store_second)


def per_device(rows_of, cols_of, contact, *weights):
    tile_rows = contact.shape[0]
    pairs = contact.shape[1] // 128
    span, all_pairs, square = tile_rows + 2 * HALO, pairs + 2 * SIDE, 2 * pairs
    fold = tile_rows // square
    buf = pltpu.VMEM((all_pairs, span, 128), jnp.bfloat16)
    return pl.pallas_call(
        functools.partial(kernel, rows_of, cols_of),
        out_shape=jax.ShapeDtypeStruct(contact.shape, jnp.bfloat16),
        in_specs=[pl.BlockSpec(memory_space=pltpu.VMEM)] * (1 + len(weights)),
        out_specs=pl.BlockSpec(memory_space=pltpu.VMEM),
        scratch_shapes=[
            buf,
            buf,
            buf,
            pltpu.VMEM((fold, pairs, square, 128), jnp.bfloat16),
            pltpu.VMEM((pairs * square, 128), jnp.float32),
            pltpu.VMEM((pairs * tile_rows, 128), jnp.float32),
            pltpu.VMEM((4, 256, 384), jnp.bfloat16),
            pltpu.VMEM((4, 384, 256), jnp.bfloat16),
            pltpu.VMEM((8, 128), jnp.float32),
            pltpu.SemaphoreType.DMA((len(WAYS),)),
            pltpu.SemaphoreType.DMA((len(WAYS),)),
            pltpu.SemaphoreType.DMA((len(WAYS),)),
            pltpu.SemaphoreType.DMA((len(WAYS),)),
            pltpu.SemaphoreType.DMA((fold,)),
            pltpu.SemaphoreType.DMA((fold,)),
            pltpu.SemaphoreType.DMA,
        ],
        compiler_params=pltpu.CompilerParams(
            collective_id=0, has_side_effects=True, vmem_limit_bytes=40 * 1024 * 1024
        ),
    )(contact, *weights)


def solution(mesh):
    in_specs = (P("row", "col"), P(), P(), P(), P(), P(), P(), P(), P())
    return jax.shard_map(
        functools.partial(per_device, mesh.shape["row"], mesh.shape["col"]),
        mesh=mesh,
        in_specs=in_specs,
        out_specs=P("row", "col"),
        check_vma=False,
    )
```

time: 124 us -> 49.7 us (0.40)
  Pallas kernels: 0 us -> 46.3 us
  waiting for transfers between devices: 31.9 us -> 0 us
  matrix products: 31.1 us -> 0 us
  starting transfers between devices: 30.3 us -> 0 us
  blocking collectives: 19.4 us -> 0 us
  local copies, waits for them, and re-layouts: 6.91 us -> 2.8 us
  other arithmetic: 2.78 us -> 0 us
    pallas_call x0 -> x1, Pallas kernels: none -> 46.3 us  [per_device(): pl.pallas_call(functools.partial(kernel, rows_of, cols_of), out_shape=jax...]
    dot_general x72 -> x0, matrix products: 31.1 us -> none  [conv_valid(): jnp.einsum('oc,crw->orw', weight[tap_row, tap_col], window, preferred_ele...]
    ppermute x8 -> x0, waiting for transfers between devices: 25.7 us -> none  [the longest x4 14.5 us: with_halo(): lax.ppermute(head, axis, [((i + 1) % count, i) for i in range(ends)])]
    ppermute x8 -> x0, starting transfers between devices: 25.2 us -> none  [the longest x4 14.2 us: with_halo(): lax.ppermute(tail, axis, [(i, (i + 1) % count) for i in range(ends)])]
    all_to_all x2 -> x0, blocking collectives: 19.4 us -> none  [the longest x1 10.4 us: mirrored(): lax.all_to_all(pieces, 'col', split_axis=2, concat_axis=3, tiled=True)]
    all_to_all x1 -> x0, waiting for transfers between devices: 6.16 us -> none  [mirrored(): lax.all_to_all(arrived, 'col', split_axis=1, concat_axis=3, tiled=True)]
    all_to_all x1 -> x0, starting transfers between devices: 5.05 us -> none  [mirrored(): lax.all_to_all(arrived, 'col', split_axis=1, concat_axis=3, tiled=True)]
    unnamed x24 -> x19, local copies, waits for them, and re-layouts: 4.26 us -> 2.8 us
  transfers between devices with their start and end apart: 9 -> 0, of which waited for: 9 -> 0; matrix products, arithmetic and copies ran while one was open for 0% -> 0% of each run, Pallas kernels for 0% -> 0%
where the time goes in v1:
time: 49.7 us; the launch traced here: 49.2 us
  Pallas kernels  46.3 us (93%)
  local copies, waits for them, and re-layouts  2.8 us (6%)
    pallas_call x1, Pallas kernels, per_device(): pl.pallas_call(functools.partial(kernel, rows_of, cols_of), out_shape=jax...  46.3 us
    unnamed x19, local copies, waits for them, and re-layouts  2.8 us

profile of v1, /device:TPU:9, one launch (start us, length us, event | category | flops | bytes accessed | tf_op | source)
XLA Modules:
  0.0 49.2 jit_solution(17640029556702843003)
XLA Ops:
  0.0 0.0 copy-start.7
  0.0 0.0 copy-start.2
  0.0 1.1 %copy.10.fu = bf16[2,3,3,64,32]{4,3,2,1,0:T(8,128)(2,1)S(1)} copy(bf16[2,3,3,64,32]{3,4,2,1,0:T(8,128)(2,1)} %param.12) | data formatting | bytes 147456 | tf_op args[3]
  1.2 0.0 copy-done.7
  1.2 0.0 copy-start
  1.2 0.0 copy-start.1
  1.2 0.0 copy-start.3
  1.2 0.0 copy-start.4
  1.2 0.0 copy-start.5
  1.2 0.0 copy-start.6
  1.2 0.2 copy.11.su
  1.4 0.0 copy-done.2
  1.5 0.7 %copy-done = bf16[64,2048]{1,0:T(8,128)(2,1)S(1)} copy-done((bf16[64,2048]{1,0:T(8,128)(2,1)S(1)}, bf16[64,2048]{1,0:T(8,128)(2,1)}, u32[]{:S(2)}) %copy-start) | copy-done | bytes 262168
  2.1 0.0 copy-done.1
  2.2 0.0 copy-done.3
  2.2 0.0 copy-done.4
  2.2 0.0 copy-done.5
  2.2 0.0 copy-done.6
  2.2 46.3 %shard_map.91 = bf16[64,2048]{1,0:T(8,128)(2,1)S(1)} custom-call(bf16[64,2048]{1,0:T(8,128)(2,1)S(1)} %copy-done, bf16[2,3,3,32,64]{4,3,2,1,0:T(8,128)(2,1)S(1)} %copy-done.1, f32[2,32]{1,0:T(2,128)S(1)} %copy-done.3, bf16[2,3,3,64,32]{4,3,2,1,0:T(8,128)(2,1)S(1)} %copy.10.fu, f32[2,64]{1,0:T(2,128)S(1)} %copy-done.4, ...), custom_call_target="tpu_custom_call" | custom-call | tf_op jit(solution)/shard_map/pallas_call | solution.py:301
  48.5 0.7 %copy.13 = bf16[64,2048]{1,0:T(8,128)(2,1)} copy(bf16[64,2048]{1,0:T(8,128)(2,1)S(1)} %shard_map.91) | data formatting | bytes 524288
Async XLA Ops:
  0.0 1.2 %copy-start.7 = (bf16[2,3,3,64,32]{3,4,2,1,0:T(8,128)(2,1)S(1)}, bf16[2,3,3,64,32]{3,4,2,1,0:T(8,128)(2,1)}, u32[]{:S(2)}) copy-start(bf16[2,3,3,64,32]{3,4,2,1,0:T(8,128)(2,1)} %param.16) | copy-start | bytes 221188
  0.0 1.4 %copy-start.2 = (bf16[2,3,3,32,64]{4,3,2,1,0:T(8,128)(2,1)S(1)}, bf16[2,3,3,32,64]{4,3,2,1,0:T(8,128)(2,1)}, u32[]{:S(2)}) copy-start(bf16[2,3,3,32,64]{4,3,2,1,0:T(8,128)(2,1)} %sd.1) | copy-start | bytes 221188
  1.2 1.0 %copy-start = (bf16[64,2048]{1,0:T(8,128)(2,1)S(1)}, bf16[64,2048]{1,0:T(8,128)(2,1)}, u32[]{:S(2)}) copy-start(bf16[64,2048]{1,0:T(8,128)(2,1)} %contact.1) | copy-start | bytes 786436
  1.2 1.0 %copy-start.1 = (bf16[2,3,3,32,64]{4,3,2,1,0:T(8,128)(2,1)S(1)}, bf16[2,3,3,32,64]{4,3,2,1,0:T(8,128)(2,1)}, u32[]{:S(2)}) copy-start(bf16[2,3,3,32,64]{4,3,2,1,0:T(8,128)(2,1)} %fd.1) | copy-start | bytes 221188
  1.2 1.0 %copy-start.3 = (f32[2,32]{1,0:T(2,128)S(1)}, f32[2,32]{1,0:T(2,128)}, u32[]{:S(2)}) copy-start(f32[2,32]{1,0:T(2,128)} %fdb.1) | copy-start | bytes 772
  1.2 1.0 %copy-start.4 = (f32[2,64]{1,0:T(2,128)S(1)}, f32[2,64]{1,0:T(2,128)}, u32[]{:S(2)}) copy-start(f32[2,64]{1,0:T(2,128)} %fub.1) | copy-start | bytes 1540
  1.2 1.0 %copy-start.5 = (f32[2,32]{1,0:T(2,128)S(1)}, f32[2,32]{1,0:T(2,128)}, u32[]{:S(2)}) copy-start(f32[2,32]{1,0:T(2,128)} %sdb.1) | copy-start | bytes 772
  1.2 0.9 %copy-start.6 = (f32[2,64]{1,0:T(2,128)S(1)}, f32[2,64]{1,0:T(2,128)}, u32[]{:S(2)}) copy-start(f32[2,64]{1,0:T(2,128)} %sub.1) | copy-start | bytes 1540
